TPU v7x, 32 devices: a whole 2x2x4 slice. The times are simulated.
32 devices in a mesh: seq: 8 (over z, y), head: 4 (over x, core).
Axes of the slice: x: 2, y: 2, z: 4, core: 2. Of those that a mesh axis runs over, the one named last changes fastest.
Arguments:
- mamba_inner: bfloat16 [1024, 3072], P('seq', 'head'), may hold values from -6 to 6
- mamba_groups: bfloat16 [1024, 512], P('seq'), may hold values from -6 to 6
- selective_gate: bfloat16 [1024, 3072], P('seq', 'head'), may hold values from -6 to 6
- step_raw: float32 [48, 1024], P('head', 'seq'), may hold values from -3 to 3
- step_bias: float32 [48], P('head'), may hold values from -0.5 to 0.5
- decay_log: float32 [48], P('head'), may hold values from -12 to -2
- conv_inner: float32 [4, 3072], P(None, 'head'), may hold values from -3 to 3
- conv_groups: float32 [4, 512], replicated, may hold values from -3 to 3
- gated_norm_gain: float32 [3072], P('head'), may hold values from 0.1 to 1.9
- query_rows: bfloat16 [1024, 1024], P('seq', 'head'), may hold values from -8 to 8
- key_rows: bfloat16 [1024, 256], P('seq'), may hold values from -8 to 8
- value_rows: bfloat16 [1024, 256], P('seq'), may hold values from -6 to 6
- segment_ids: int32 [1024], P('seq'), may hold values from 0 to 15, never falling along the last dimension, each value on 1 to 682 neighbouring positions
- mamba_proj: bfloat16 [3072, 2048], P('head'), may hold values from -0.109375 to 0.109375
- attn_proj: bfloat16 [1024, 2048], P('head'), may hold values from -0.1875 to 0.1875
Outputs:
- mixed: bfloat16 [1024, 2048], P('seq', 'head')
Inputs may be any that keep to these rules, and one draw needn't show every extreme that they name: `segment_ids`: prompt numbers never fall along the tokens; each prompt holds 1 to 682 tokens and one holds exactly 682.
All inputs are finite; a program needn't handle non-finite values.
Results may differ from a plain program's by a relative error of at most 0.015.
Values may be sent and summed in bfloat16 or wider, within the bound.
A program may use at most 128 MiB of HBM per device.

v0:
```python
import math
import jax
import jax.numpy as jnp
from jax import lax
from jax.sharding import PartitionSpec as P

HEAD_CHANNELS = 64
STATE_SIZE = 256
QH = 8
KVH = 2
HD = 128


def shifted(value, axis, steps):
    count = lax.axis_size(axis)
    first, last = (max(0, -steps), min(count, count - steps))
    return lax.ppermute(value, axis, [(source, source + steps) for source in range(first, last)])


def entering(array, axis, combine, identity):
    length, position = (lax.axis_size(axis), lax.axis_index(axis))
    everything = jax.tree.map(
        lambda part, kind: lax.all_gather(part.astype(kind), axis),
        array,
        (jnp.bfloat16, jnp.bfloat16),
    )
    start = jax.tree.map(
        lambda part, zero: jnp.broadcast_to(jnp.asarray(zero, part.dtype), part.shape),
        array,
        identity,
    )

    def turn(k, before):
        reached = k < position
        new = combine(
            before, jax.tree.map(lambda part, own: part[k].astype(own.dtype), everything, array)
        )
        return jax.tree.map(lambda a, b: jnp.where(reached, a, b), new, before)

    return lax.fori_loop(0, length, turn, start)


def conv_silu(rows, weight, segs, rim_rows, rim_segs):
    item_count = rows.shape[0]
    padded = jnp.concatenate([rim_rows.astype(jnp.float32), rows.astype(jnp.float32)], 0)
    seg_pad = jnp.concatenate([rim_segs, segs], 0)
    total = jnp.zeros(rows.shape, jnp.float32)
    for offset in range(weight.shape[0]):
        window = padded[offset : offset + item_count]
        keep = (seg_pad[offset : offset + item_count] == segs).astype(jnp.float32)
        total = total + weight[offset][None, :] * window * keep[:, None]
    return jax.nn.silu(total).astype(jnp.bfloat16)


def mamba_local(inner, groups, segs, steps, rates, prev_last):
    highest = lax.Precision.HIGHEST
    cumul = jnp.cumsum(-steps * rates[:, None], axis=1)
    read_b = groups[:, :STATE_SIZE]
    read_c = groups[:, STATE_SIZE:]
    intersection = jnp.dot(read_c, read_b.T, preferred_element_type=jnp.float32)
    order = jnp.arange(segs.shape[0], dtype=jnp.int32)
    live = (segs[:, None] == segs[None, :]) & (order[:, None] >= order[None, :])
    decays = jnp.exp(jnp.where(live[None], cumul[:, :, None] - cumul[:, None, :], -jnp.inf))
    mixing = intersection[None] * decays
    scaled = inner.astype(jnp.float32) * steps.T[:, :, None]
    output = jnp.einsum("htj,jhd->thd", mixing, scaled, precision=highest)
    tail = jnp.exp(cumul[:, -1:] - cumul) * (segs == segs[-1]).astype(jnp.float32)[None, :]
    local_state = jnp.einsum(
        "ht,thd,tn->hdn", tail, scaled, read_b.astype(jnp.float32), precision=highest
    )
    through = jnp.exp(cumul[:, -1]) * (segs[-1] == prev_last).astype(jnp.float32)
    return (output, through, local_state, cumul)


def mamba_incoming(output, incoming, groups, segs, cumul, prev_last):
    read_c = groups[:, STATE_SIZE:].astype(jnp.float32)
    joined = (segs == prev_last).astype(jnp.float32)
    from_carry = jnp.einsum("hdn,tn->thd", incoming, read_c, precision=lax.Precision.HIGHEST)
    return output + jnp.exp(cumul).T[:, :, None] * joined[:, None, None] * from_carry


def combine_states(earlier, later):
    return (earlier[0] * later[0], later[0][:, None, None] * earlier[1] + later[1])


def shards(
    mamba_inner,
    mamba_groups,
    selective_gate,
    step_raw,
    step_bias,
    decay_log,
    conv_inner,
    conv_groups,
    gated_norm_gain,
    query_rows,
    key_rows,
    value_rows,
    segment_ids,
    mamba_proj,
    attn_proj,
):
    item_count = segment_ids.shape[0]
    taps = conv_inner.shape[0]
    resident_heads = step_raw.shape[0]
    rim_inner, rim_groups, rim_marks = shifted(
        (
            mamba_inner[item_count - taps + 1 :],
            mamba_groups[item_count - taps + 1 :],
            segment_ids[item_count - taps + 1 :].astype(jnp.bfloat16),
        ),
        "seq",
        1,
    )
    rim_segs = rim_marks.astype(jnp.float32).astype(jnp.int32)
    prev_last = rim_segs[-1]
    inner_filtered = conv_silu(mamba_inner, conv_inner, segment_ids, rim_inner, rim_segs).reshape(
        item_count, resident_heads, HEAD_CHANNELS
    )
    groups_conv = conv_silu(mamba_groups, conv_groups, segment_ids, rim_groups, rim_segs)
    steps = jax.nn.softplus(step_raw + step_bias[:, None])
    rates = jnp.exp(decay_log)
    output, through, local_state, cumul = mamba_local(
        inner_filtered, groups_conv, segment_ids, steps, rates, prev_last
    )
    identity = (jnp.ones_like(through), jnp.zeros_like(local_state))
    carry_decay, carry_state = entering((through, local_state), "seq", combine_states, identity)
    selective_output = mamba_incoming(
        output, carry_state, groups_conv, segment_ids, cumul, prev_last
    )
    gated_values = selective_output * jax.nn.silu(selective_gate.astype(jnp.float32)).reshape(
        item_count, resident_heads, HEAD_CHANNELS
    )
    mean_square = jnp.mean(gated_values * gated_values, axis=-1, keepdims=True)
    normalized_rows = (
        (
            gated_values
            * lax.rsqrt(mean_square + 1e-05)
            * gated_norm_gain.reshape(resident_heads, HEAD_CHANNELS)
        )
        .astype(jnp.bfloat16)
        .reshape(item_count, resident_heads * HEAD_CHANNELS)
    )
    heads_here = query_rows.shape[1] // HD
    group_size = QH // KVH
    kv_index = lax.axis_index("head") * heads_here // group_size
    my_keys = lax.dynamic_slice_in_dim(key_rows, kv_index * HD, HD, 1)
    my_values = lax.dynamic_slice_in_dim(value_rows, kv_index * HD, HD, 1)
    marks = segment_ids.astype(jnp.bfloat16)
    block_start = lax.axis_index("seq") * item_count
    query_pos = block_start + jnp.arange(item_count, dtype=jnp.int32)
    queries = query_rows.reshape(item_count, heads_here, HD).transpose(1, 0, 2)
    scale = 1.0 / math.sqrt(HD)
    start_state = (
        jnp.full((heads_here, item_count), -1e30, jnp.float32),
        jnp.zeros((heads_here, item_count), jnp.float32),
        jnp.zeros((heads_here, item_count, HD), jnp.float32),
    )
    piece_keys = lax.all_gather(my_keys, "seq", axis=0, tiled=True)
    piece_values = lax.all_gather(my_values, "seq", axis=0, tiled=True)
    piece_marks = lax.all_gather(marks, "seq", axis=0, tiled=True)
    rows = piece_keys.shape[0]
    width = math.gcd(rows, item_count)
    blocks = rows // width

    def one_block(state, item):
        top, total, summed = state
        block_keys, block_values, block_marks, offset = item
        key_pos = offset * width + jnp.arange(width, dtype=jnp.int32)
        key_seg = block_marks.astype(jnp.float32).astype(jnp.int32)
        allowed = (
            (key_seg[None, :] == segment_ids[:, None])
            & (key_pos[None, :] <= query_pos[:, None])
            & (key_pos[None, :] >= 0)
        )
        scores = (
            jnp.einsum("hqd,kd->hqk", queries, block_keys, preferred_element_type=jnp.float32)
            * scale
        )
        scores = jnp.where(allowed[None], scores, -jnp.inf)
        new_top = jnp.maximum(top, jnp.max(scores, axis=-1))
        rescale = jnp.exp(top - new_top)
        weights = jnp.exp(scores - new_top[..., None])
        total = total * rescale + jnp.sum(weights, axis=-1)
        summed = summed * rescale[..., None] + jnp.einsum(
            "hqk,kd->hqd",
            weights.astype(jnp.bfloat16),
            block_values,
            preferred_element_type=jnp.float32,
        )
        return ((new_top, total, summed), None)

    items = (
        piece_keys.reshape(blocks, width, HD),
        piece_values.reshape(blocks, width, HD),
        piece_marks.reshape(blocks, width),
        jnp.arange(blocks, dtype=jnp.int32),
    )
    result, unused = lax.scan(one_block, start_state, items)
    top_final, total_final, summed_final = result
    attended = (
        (summed_final / total_final[..., None])
        .astype(jnp.bfloat16)
        .transpose(1, 0, 2)
        .reshape(item_count, heads_here * HD)
    )
    terms = jnp.dot(normalized_rows, mamba_proj, preferred_element_type=jnp.float32) + jnp.dot(
        attended, attn_proj, preferred_element_type=jnp.float32
    )
    return lax.psum_scatter(terms.astype(jnp.bfloat16), "head", scatter_dimension=1, tiled=True)


def solution(mesh):
    placed = (
        P("seq", "head"),
        P("seq", None),
        P("seq", "head"),
        P("head", "seq"),
        P("head"),
        P("head"),
        P(None, "head"),
        P(),
        P("head"),
        P("seq", "head"),
        P("seq", None),
        P("seq", None),
        P("seq"),
        P("head", None),
        P("head", None),
    )
    return jax.shard_map(
        shards, mesh=mesh, in_specs=placed, out_specs=P("seq", "head"), check_vma=False
    )
```

profile of v0, /device:TPU:0, one launch (start us, length us, event | category | flops | bytes accessed | tf_op | source)
XLA Modules:
  0.0 241.9 jit_solution(1705443980735956197)
XLA Ops:
  6.5 0.8 fusion.75
  7.9 5.4 %collective-permute-start.1 = (bf16[3]{0:T(256)(128)(2,1)}, bf16[3]{0:T(256)(128)(2,1)}, u32[]{:S(2)}, u32[]{:S(2)}) collective-permute-start(bf16[3]{0:T(256)(128)(2,1)} %slice.85), channel_id=1, source_target_pairs={{0,4},{4,8},{8,12},{12,16},{16,20},{20,24},{24,28},{1,5},{5,9},{9,... | collective-permute-start | bytes 26 | tf_op jit(solution)/shard_map/ppermute | solution.py:17
  13.3 0.7 slice.95
  14.0 3.5 %collective-permute-start.2 = (bf16[3,512]{1,0:T(4,128)(2,1)S(1)}, bf16[3,512]{1,0:T(4,128)(2,1)}, u32[]{:S(2)}, u32[]{:S(2)}) collective-permute-start(bf16[3,512]{1,0:T(4,128)(2,1)S(1)} %slice.95), channel_id=1, source_target_pairs={{0,4},{4,8},{8,12},{12,16},{16,20},{20,24},{24,28},{1,5},{5,9},{9,... | collective-permute-start | bytes 9224 | tf_op jit(solution)/shard_map/ppermute | solution.py:17
  17.5 0.7 slice.83
  18.2 0.8 copy.27
  19.1 3.5 %collective-permute-start = (bf16[3,768]{0,1:T(8,128)(2,1)}, bf16[3,768]{0,1:T(8,128)(2,1)}, u32[]{:S(2)}, u32[]{:S(2)}) collective-permute-start(bf16[3,768]{0,1:T(8,128)(2,1)} %copy.27), channel_id=1, source_target_pairs={{0,4},{4,8},{8,12},{12,16},{16,20},{20,24},{24,28},{1,5},{5,9},{9,... | collective-permute-start | bytes 13832 | tf_op jit(solution)/shard_map/ppermute | solution.py:17
  22.6 1.2 slice.106
  23.8 1.6 convert_element_type.131
  25.5 1.1 copy.28
  26.6 0.9 fusion.74
  27.5 0.9 slice_reduce_fusion.4
  28.4 0.8 convert_element_type.121
  29.8 0.8 fusion.71
  31.1 0.8 constant_dynamic-slice_fusion.2
  31.8 32.9 %all_gather.23 = bf16[1024,128]{1,0:T(8,128)(2,1)} all-gather(bf16[128,128]{1,0:T(8,128)(2,1)S(1)} %constant_dynamic-slice_fusion.2), channel_id=1, replica_groups=mesh['seq'=8,'head'=4] {'seq'}, dimensions={0}, use_global_device_ids=true | all-gather | bytes 294912 | tf_op jit(solution)/shard_map/all_gather | solution.py:159
  64.8 0.8 constant_dynamic-slice_fusion.1
  65.5 32.9 %all_gather.24 = bf16[1024,128]{1,0:T(8,128)(2,1)} all-gather(bf16[128,128]{1,0:T(8,128)(2,1)S(1)} %constant_dynamic-slice_fusion.1), channel_id=1, replica_groups=mesh['seq'=8,'head'=4] {'seq'}, dimensions={0}, use_global_device_ids=true | all-gather | bytes 294912 | tf_op jit(solution)/shard_map/all_gather | solution.py:160
  98.4 16.8 %all-gather.2 = bf16[8,1,128]{2,1,0:T(2,128)(2,1)S(1)} all-gather(bf16[1,1,128]{2,1,0:T(2,128)(2,1)S(1)} %get-tuple-element.295), channel_id=1, replica_groups=mesh['seq'=8,'head'=4] {'seq'}, dimensions={0}, use_global_device_ids=true | all-gather | bytes 2304 | tf_op jit(solution)/shard_map/all_gather | solution.py:161
  115.8 0.9 copy.30
  118.1 0.7 pad_add_fusion
  118.8 2.0 compare_convert_fusion.4
  122.1 1.6 multiply_convert_fusion.2
  123.7 1.0 convert_element_type.120
  124.7 2.5 %multiply_convert_fusion.1 = bf16[128,768]{0,1:T(8,128)(2,1)S(1)} fusion(f32[128,768]{0,1:T(8,128)} %convert_element_type.121, f32[3,768]{0,1:T(8,128)S(1)} %convert_element_type.120, f32[768]{0:T(1024)S(1)} %get-tuple-element.241, f32[128]{0:T(128)S(1)} %get-tuple-element.290, f32[768]{0:T(1024)S(1)} %get-tuple-element.242, f32[128]{0:T(128)S(1)} %get-tuple-element.291, ...), kind=kLoop, calls=%fused_computation.74 | loop fusion | flops 1769472 | bytes 612864 | tf_op jit(solution)/shard_map/convert_element_type | solution.py:52
  127.9 1.2 convolution_convert_fusion
  129.2 32.5 %while.30 = (s32[]{:T(128)}, f32[2,128]{1,0:T(2,128)S(1)}, f32[2,128]{1,0:T(2,128)S(1)}, f32[2,128,128]{2,1,0:T(8,128)S(1)}, bf16[8,128]{1,0:T(8,128)(2,1)}, /*i...) while((s32[]{:T(128)}, f32[2,128]{1,0:T(2,128)S(1)}, ...), condition=%wide.region_7.8_spmd.clone, body=%wide.region_4.7_spmd.clone.sunk | while | flops 17172484 | bytes 840889 | solution.py:199
  130.4 0.7 fusion.96
  131.2 0.9 fusion.97
  132.2 1.0 convolution_add_fusion.3
  134.5 0.7 fusion.96
  135.3 0.9 fusion.97
  136.3 1.0 convolution_add_fusion.3
  139.3 0.9 fusion.97
  140.4 1.0 convolution_add_fusion.3
  143.4 0.9 fusion.97
  144.4 1.0 convolution_add_fusion.3
  146.6 0.7 fusion.96
  147.4 0.9 fusion.97
  148.5 1.0 convolution_add_fusion.3
  151.5 0.9 fusion.97
  152.5 1.0 convolution_add_fusion.3
  155.6 0.9 fusion.97
  156.6 1.0 convolution_add_fusion.3
  159.6 1.0 fusion.97
  160.7 1.0 convolution_add_fusion.3
  161.7 1.8 copy.29
  164.3 1.3 dynamic-slice
  166.4 1.8 convert_multiply_fusion
  168.2 2.6 %fusion.76 = f32[128,2048]{1,0:T(8,128)} fusion(bf16[128,256]{0,1:T(8,128)(2,1)S(1)} %bitcast.93, bf16[256,2048]{1,0:T(8,128)(2,1)} %param.33), kind=kOutput, calls=%fused_computation.132 | convolution fusion | flops 134217728 | bytes 2162688 | tf_op jit(solution)/shard_map/dot_general | solution.py:207
  172.5 18.7 %all-reduce = bf16[96]{0:T(256)(128)(2,1)S(1)} all-reduce(bf16[96]{0:T(256)(128)(2,1)S(1)} %dynamic-update-slice), channel_id=2, replica_groups=mesh['seq'=8,'head'=4] {'seq'}, use_global_device_ids=true, to_apply=%add | all-reduce | flops 96 | bytes 384
  191.4 18.2 %while.29 = (s32[]{:T(128)}, f32[12,64,256]{2,1,0:T(8,128)}, s32[]{:T(128)}, bf16[8,12]{1,0:T(8,128)(2,1)S(1)}, bf16[8,12,64,256]{3,2,1,0:T(8,128)(2,1)}, /*index=5*/s32[]{:T(128)}, s32[]{:T(128)}) while((s32[]{:T(128)}, f32[12,64,256]{2,1,0:T(8,128)}, s32[]{:T(128)}, bf16[8,12]{1,0:T(8,128)(2,1)S(1)}, ...), condition=%wide.region_2.3_spmd.clone, body=%wide.region_1.2_spmd.clone.sunk | while | flops 983056 | bytes 1966305 | solution.py:40
  191.5 2.1 fusion.92
  193.5 2.3 fusion.92
  195.8 2.3 fusion.92
  198.1 2.3 fusion.92
  200.4 2.3 fusion.92
  202.7 2.3 fusion.92
  205.0 2.3 fusion.92
  207.3 2.3 fusion.92
  209.6 1.7 convolution_multiply_fusion.1
  211.3 2.8 %multiply_reduce_fusion = (f32[128,12]{0,1:T(8,128)S(1)}, f32[128,12,64]{0,2,1:T(8,128)S(1)}) fusion(f32[128,12,64]{0,2,1:T(8,128)} %bitcast.92, f32[128,12,64]{0,2,1:T(8,128)S(1)} %convolution_multiply_fusion.1, f32[12,128]{1,0:T(8,128)S(1)} %reduce_window_sum.11, f32[128,128]{1,0:T(8,128)S(1)} %fusion.66, pred[128,128]{1,0:T(8,128)(4,1)S(1)} %fusion.64, ...), kind=kOutput, calls=%fused_computation.69 | convolution fusion | flops 152173056 | bytes 1476608 | tf_op jit(solution)/shard_map/htj,jhd->thd/dot_general | solution.py:66
  214.4 1.4 fusion.20
  215.8 19.3 %reduce-scatter.2.cloned.1.call-done = bf16[128,512]{1,0:T(8,128)(2,1)} async-done(((bf16[128,2048]{1,0:T(8,128)(2,1)}), bf16[128,512]{1,0:T(8,128)(2,1)}) %reduce-scatter.2.cloned.1.call-update) | async-done | bytes 131088 | tf_op jit(solution)/shard_map/reduce_scatter | solution.py:210
  (133 shorter events, 17.3 us)
Async XLA Ops:
  6.5 207.8 %copy-start = (bf16[768,2048]{1,0:T(8,128)(2,1)S(1)}, bf16[768,2048]{1,0:T(8,128)(2,1)}, u32[]{:S(2)}) copy-start(bf16[768,2048]{1,0:T(8,128)(2,1)} %param.32) | copy-start | bytes 9437188
  6.5 122.6 %copy-start.5 = (s32[128]{0:T(128)S(1)}, s32[128]{0:T(128)}, u32[]{:S(2)}) copy-start(s32[128]{0:T(128)} %param.31) | copy-start | bytes 1540
  6.5 184.9 %all-gather.5.cloned.1.call-start = ((), (), s32[]{:S(2)}) async-start(), calls=%async_computation.2 | async-start | bytes 3538944 | tf_op jit(solution)/shard_map/all_gather | solution.py:23
  7.9 108.9 %collective-permute-start.1 = (bf16[3]{0:T(256)(128)(2,1)}, bf16[3]{0:T(256)(128)(2,1)}, u32[]{:S(2)}, u32[]{:S(2)}) collective-permute-start(bf16[3]{0:T(256)(128)(2,1)} %slice.85), channel_id=1, source_target_pairs={{0,4},{4,8},{8,12},{12,16},{16,20},{20,24},{24,28},{1,5},{5,9},{9,... | collective-permute-start | bytes 26 | tf_op jit(solution)/shard_map/ppermute | solution.py:17
  14.0 107.4 %collective-permute-start.2 = (bf16[3,512]{1,0:T(4,128)(2,1)S(1)}, bf16[3,512]{1,0:T(4,128)(2,1)}, u32[]{:S(2)}, u32[]{:S(2)}) collective-permute-start(bf16[3,512]{1,0:T(4,128)(2,1)S(1)} %slice.95), channel_id=1, source_target_pairs={{0,4},{4,8},{8,12},{12,16},{16,20},{20,24},{24,28},{1,5},{5,9},{9,... | collective-permute-start | bytes 9224 | tf_op jit(solution)/shard_map/ppermute | solution.py:17
  19.1 104.6 %collective-permute-start = (bf16[3,768]{0,1:T(8,128)(2,1)}, bf16[3,768]{0,1:T(8,128)(2,1)}, u32[]{:S(2)}, u32[]{:S(2)}) collective-permute-start(bf16[3,768]{0,1:T(8,128)(2,1)} %copy.27), channel_id=1, source_target_pairs={{0,4},{4,8},{8,12},{12,16},{16,20},{20,24},{24,28},{1,5},{5,9},{9,... | collective-permute-start | bytes 13832 | tf_op jit(solution)/shard_map/ppermute | solution.py:17
  30.6 98.6 %copy-start.6 = (f32[128,12]{0,1:T(8,128)}, f32[128,12]{0,1:T(8,128)S(1)}, u32[]{:S(2)}) copy-start(f32[128,12]{0,1:T(8,128)S(1)} %get-tuple-element.281) | copy-start | bytes 18436
  123.7 3.5 %copy-start.2 = (bf16[128,512]{1,0:T(8,128)(2,1)}, bf16[128,512]{1,0:T(8,128)(2,1)S(1)}, u32[]{:S(2)}) copy-start(bf16[128,512]{1,0:T(8,128)(2,1)S(1)} %multiply_convert_fusion.2) | copy-start | bytes 393220
  127.2 0.7 copy-start.4
  127.2 36.3 %copy-start.10 = (f32[768]{0:T(1024)S(1)}, f32[768]{0:T(1024)}, u32[]{:S(2)}) copy-start(f32[768]{0:T(1024)} %param.27) | copy-start | bytes 9220
  129.1 106.0 %reduce-scatter.2.cloned.1.call-start = ((), (), s32[]{:S(2)}) async-start(), calls=%async_computation.1 | async-start | bytes 655360 | tf_op jit(solution)/shard_map/reduce_scatter | solution.py:210
  161.7 29.6 %copy-start.3 = (bf16[128,512]{1,0:T(8,128)(2,1)S(1)}, bf16[128,512]{1,0:T(8,128)(2,1)}, u32[]{:S(2)}) copy-start(bf16[128,512]{1,0:T(8,128)(2,1)} %copy-done.2) | copy-start | bytes 393220
  191.4 18.2 %copy-start.8 = (f32[128,12]{0,1:T(8,128)S(1)}, f32[128,12]{0,1:T(8,128)}, u32[]{:S(2)}) copy-start(f32[128,12]{0,1:T(8,128)} %get-tuple-element.283) | copy-start | bytes 18436
  191.4 19.9 %copy-start.7 = (f32[128,12]{0,1:T(8,128)S(1)}, f32[128,12]{0,1:T(8,128)}, u32[]{:S(2)}) copy-start(f32[128,12]{0,1:T(8,128)} %copy-done.6) | copy-start | bytes 18436
  191.4 22.7 %copy-start.9 = (f32[12,64]{1,0:T(8,128)S(1)}, f32[12,64]{1,0:T(8,128)}, u32[]{:S(2)}) copy-start(f32[12,64]{1,0:T(8,128)} %mul.345) | copy-start | bytes 9220
  209.6 4.7 %copy-start.1 = (f32[128,2048]{1,0:T(8,128)S(1)}, f32[128,2048]{1,0:T(8,128)}, u32[]{:S(2)}) copy-start(f32[128,2048]{1,0:T(8,128)} %fusion.76) | copy-start | bytes 3145732
Sparse Core Ops, SparseCore 0:
  129.2 58.6 all-gather.4
  215.9 19.1 reduce-scatter.1
where the time goes:
time: 244 us; the launch traced here: 242 us
  blocking collectives  101 us (41%)
  other arithmetic  41.5 us (17%)
  matrix products  25.3 us (10%)
  local copies, waits for them, and re-layouts  21.2 us (9%)
  waiting for transfers between devices  19.4 us (8%)
  between operations  15.7 us (6%)
  starting transfers between devices  12.4 us (5%)
  loops' own time  5.2 us (2%)
    all_gather x1, blocking collectives, shards(): piece_keys = lax.all_gather(my_keys, 'seq', axis=0, tiled=True)  32.9 us
    all_gather x1, blocking collectives, shards(): piece_values = lax.all_gather(my_values, 'seq', axis=0, tiled=True)  32.9 us
    reduce_scatter x1, waiting for transfers between devices, shards(): lax.psum_scatter(terms.astype(jnp.bfloat16), 'head', scatter_dimension=1,...  19.3 us
    unnamed x1, blocking collectives  18.7 us
    select_n x8, other arithmetic, turn(): return jax.tree.map(lambda a, b: jnp.where(reached, a, b), new, before)  18.1 us
    all_gather x1, blocking collectives, shards(): piece_marks = lax.all_gather(marks, 'seq', axis=0, tiled=True)  16.8 us
    ppermute x3, starting transfers between devices, shifted(): lax.ppermute(value, axis, [(source, source + steps) for source in range(f...  12.4 us
    dot_general x8, matrix products, one_block(): jnp.einsum('hqk,kd->hqd', weights.astype(jnp.bfloat16), block_values, pre...  7.87 us
  transfers between devices with their start and end apart: 5, of which 1 were waited for; matrix products, arithmetic and copies ran while one was open for 24% of the time, Pallas kernels for 0%

commit v1 on v0

--- a/solution.py
+++ b/solution.py
@@ -157,7 +157,27 @@
         jnp.zeros((heads_here, item_count, HD), jnp.float32),
     )
     piece_keys = lax.all_gather(my_keys, "seq", axis=0, tiled=True)
-    piece_values = lax.all_gather(my_values, "seq", axis=0, tiled=True)
+    peers, position_2, width_2 = (lax.axis_size("seq"), lax.axis_index("seq"), my_values.shape[0])
+    forward = [(i, (i + 1) % peers) for i in range(peers)]
+    left = [(i, (i - 1) % peers) for i in range(peers)]
+    piece_values = jnp.zeros(
+        (*my_values.shape[:0], peers * width_2, *my_values.shape[0 + 1 :]), my_values.dtype
+    )
+    piece_values = lax.dynamic_update_slice_in_dim(
+        piece_values, my_values, position_2 * width_2, axis=0
+    )
+    from_left = from_right = my_values
+    middle = peers // 2
+    for step in range(1, middle + 1):
+        from_left = lax.ppermute(from_left, "seq", forward)
+        piece_values = lax.dynamic_update_slice_in_dim(
+            piece_values, from_left, (position_2 - step) % peers * width_2, axis=0
+        )
+        if step < peers - middle:
+            from_right = lax.ppermute(from_right, "seq", left)
+            piece_values = lax.dynamic_update_slice_in_dim(
+                piece_values, from_right, (position_2 + step) % peers * width_2, axis=0
+            )
     piece_marks = lax.all_gather(marks, "seq", axis=0, tiled=True)
     rows = piece_keys.shape[0]
     width = math.gcd(rows, item_count)

time: 244 us -> 274 us (1.12)
  blocking collectives: 101 us -> 68.2 us
  other arithmetic: 41.5 us -> 69 us
  local copies, waits for them, and re-layouts: 21.2 us -> 36.3 us
  starting transfers between devices: 12.4 us -> 24 us
  waiting for transfers between devices: 19.4 us -> 26.4 us
    all_gather x1 -> x0, blocking collectives: 32.9 us -> none  [shards(): piece_values = lax.all_gather(my_values, 'seq', axis=0, tiled=True)]
    ppermute x0 -> x7, starting transfers between devices: none -> 15.5 us  [the longest x3 10.7 us: shards(): from_right = lax.ppermute(from_right, 'seq', left)]
    add x8, other arithmetic: 0.14 us -> 9.68 us  [one_block(): total = total * rescale + jnp.sum(weights, axis=-1)]
    convert_element_type x8, other arithmetic: 0.04 us -> 9.35 us  [turn(): part[k].astype(own.dtype)]
    dynamic_update_slice x0 -> x8, local copies, waits for them, and re-layouts: none -> 7.32 us  [the longest x4 3.19 us: shards(): lax.dynamic_update_slice_in_dim(piece_values, from_left, (position_2 - st...]
    ppermute x0 -> x7, waiting for transfers between devices: none -> 7.28 us  [the longest x4 7.27 us: shards(): from_left = lax.ppermute(from_left, 'seq', forward)]
    and x8, other arithmetic: 0.96 us -> 6.16 us  [one_block(): (key_seg[None, :] == segment_ids[:, None]) & (key_pos[None, :] <= query_p...]
    dynamic_slice x8, local copies, waits for them, and re-layouts: 4.73 us -> 9.82 us  [shards(): result, unused = lax.scan(one_block, start_state, items)]
  transfers between devices with their start and end apart: 5 -> 12, of which waited for: 1 -> 3; matrix products, arithmetic and copies ran while one was open for 24% -> 35% of each run, Pallas kernels for 0% -> 0%
where the time goes in v1:
time: 274 us; the launch traced here: 271 us
  other arithmetic  69 us (25%)
  blocking collectives  68.2 us (25%)
  local copies, waits for them, and re-layouts  36.3 us (13%)
  waiting for transfers between devices  26.4 us (10%)
  matrix products  25.8 us (9%)
  starting transfers between devices  24 us (9%)
  between operations  15.7 us (6%)
  loops' own time  5.47 us (2%)
    all_gather x1, blocking collectives, shards(): piece_keys = lax.all_gather(my_keys, 'seq', axis=0, tiled=True)  32.8 us
    reduce_scatter x1, waiting for transfers between devices, shards(): lax.psum_scatter(terms.astype(jnp.bfloat16), 'head', scatter_dimension=1,...  19 us
    select_n x8, other arithmetic, turn(): return jax.tree.map(lambda a, b: jnp.where(reached, a, b), new, before)  18.3 us
    all_gather x1, blocking collectives, shards(): piece_marks = lax.all_gather(marks, 'seq', axis=0, tiled=True)  18 us
    unnamed x1, blocking collectives  17.4 us
    ppermute x3, starting transfers between devices, shards(): from_right = lax.ppermute(from_right, 'seq', left)  10.7 us
    dynamic_slice x8, local copies, waits for them, and re-layouts, shards(): result, unused = lax.scan(one_block, start_state, items)  9.82 us
    add x8, other arithmetic, one_block(): total = total * rescale + jnp.sum(weights, axis=-1)  9.68 us
  transfers between devices with their start and end apart: 12, of which 3 were waited for; matrix products, arithmetic and copies ran while one was open for 35% of the time, Pallas kernels for 0%

profile of v1, /device:TPU:0, one launch (start us, length us, event | category | flops | bytes accessed | tf_op | source)
XLA Modules:
  0.0 270.8 jit_solution(12767234549833551922)
XLA Ops:
  7.3 1.6 constant_dynamic-update-slice_fusion.7
  8.8 3.0 %collective-permute-start.3 = (bf16[128,128]{1,0:T(8,128)(2,1)}, bf16[128,128]{1,0:T(8,128)(2,1)}, u32[]{:S(2)}, u32[]{:S(2)}) collective-permute-start(bf16[128,128]{1,0:T(8,128)(2,1)} %get-tuple-element.278), channel_id=1, source_target_pairs={{0,4},{4,8},{8,12},{12,16},{16,20},{20,24},{24,28},{28,0},{1,5},{5... | collective-permute-start | bytes 98312 | tf_op jit(solution)/shard_map/ppermute | solution.py:172
  11.8 3.0 %collective-permute-start.4 = (bf16[128,128]{1,0:T(8,128)(2,1)}, bf16[128,128]{1,0:T(8,128)(2,1)}, u32[]{:S(2)}, u32[]{:S(2)}) collective-permute-start(bf16[128,128]{1,0:T(8,128)(2,1)} %get-tuple-element.278), channel_id=1, source_target_pairs={{0,28},{4,0},{8,4},{12,8},{16,12},{20,16},{24,20},{28,24},{1,29},{... | collective-permute-start | bytes 98312 | tf_op jit(solution)/shard_map/ppermute | solution.py:177
  14.8 1.2 fusion.75
  16.7 1.8 collective-permute-start.1
  18.5 1.3 slice.95
  19.8 4.0 %collective-permute-start.2 = (bf16[3,512]{1,0:T(4,128)(2,1)}, bf16[3,512]{1,0:T(4,128)(2,1)}, u32[]{:S(2)}, u32[]{:S(2)}) collective-permute-start(bf16[3,512]{1,0:T(4,128)(2,1)} %slice.95), channel_id=1, source_target_pairs={{0,4},{4,8},{8,12},{12,16},{16,20},{20,24},{24,28},{1,5},{5,9},{9,... | collective-permute-start | bytes 9224 | tf_op jit(solution)/shard_map/ppermute | solution.py:17
  25.4 2.6 collective-permute-start
  28.0 1.2 slice.106
  29.2 1.6 convert_element_type.131
  32.0 1.4 fusion.64
  33.4 1.5 fusion.74
  34.8 1.5 slice_reduce_fusion.4
  37.8 1.4 fusion.71
  42.1 1.3 mul.367
  44.2 32.8 %all_gather.20 = bf16[1024,128]{1,0:T(8,128)(2,1)} all-gather(bf16[128,128]{1,0:T(8,128)(2,1)S(1)} %constant_dynamic-slice_fusion.2), channel_id=1, replica_groups=mesh['seq'=8,'head'=4] {'seq'}, dimensions={0}, use_global_device_ids=true | all-gather | bytes 294912 | tf_op jit(solution)/shard_map/all_gather | solution.py:159
  77.0 18.0 %all-gather.2 = bf16[8,1,128]{2,1,0:T(2,128)(2,1)S(1)} all-gather(bf16[1,1,128]{2,1,0:T(2,128)(2,1)} %get-tuple-element.297), channel_id=1, replica_groups=mesh['seq'=8,'head'=4] {'seq'}, dimensions={0}, use_global_device_ids=true | all-gather | bytes 2304 | tf_op jit(solution)/shard_map/all_gather | solution.py:181
  95.9 1.3 dynamic-slice
  101.3 2.0 compare_convert_fusion.4
  103.3 1.3 multiply_bitcast_fusion.1
  105.0 17.4 %all-reduce = bf16[96]{0:T(256)(128)(2,1)S(1)} all-reduce(bf16[96]{0:T(256)(128)(2,1)S(1)} %dynamic-update-slice), channel_id=2, replica_groups=mesh['seq'=8,'head'=4] {'seq'}, use_global_device_ids=true, to_apply=%add | all-reduce | flops 96 | bytes 384
  123.7 1.5 multiply_convert_fusion.2
  126.3 2.5 multiply_convert_fusion.1
  129.5 1.9 convolution_convert_fusion
  131.5 1.9 collective-permute-start.5
  133.4 2.9 %collective-permute-start.6 = (bf16[128,128]{1,0:T(8,128)(2,1)}, bf16[128,128]{1,0:T(8,128)(2,1)S(1)}, u32[]{:S(2)}, u32[]{:S(2)}) collective-permute-start(bf16[128,128]{1,0:T(8,128)(2,1)} %collective-permute-done.4), channel_id=1, source_target_pairs={{0,28},{4,0},{8,4},{12,8},{16,12},{20,16},{24,20},{28,24},{1,29},{... | collective-permute-start | bytes 98312 | tf_op jit(solution)/shard_map/ppermute | solution.py:177
  136.3 1.4 constant_dynamic-update-slice_fusion.6
  137.7 1.4 constant_dynamic-update-slice_fusion.5
  139.1 4.7 %collective-permute-start.8 = (bf16[128,128]{1,0:T(8,128)(2,1)S(1)}, bf16[128,128]{1,0:T(8,128)(2,1)S(1)}, u32[]{:S(2)}, u32[]{:S(2)}) collective-permute-start(bf16[128,128]{1,0:T(8,128)(2,1)S(1)} %collective-permute-done.6), channel_id=1, source_target_pairs={{0,28},{4,0},{8,4},{12,8},{16,12},{20,16},{24,20},{28,24},{1,29},{... | collective-permute-start | bytes 98312 | tf_op jit(solution)/shard_map/ppermute | solution.py:177
  145.0 1.2 collective-permute-done.7
  147.4 6.1 %collective-permute-done.9 = bf16[128,128]{1,0:T(8,128)(2,1)S(1)} collective-permute-done((bf16[128,128]{1,0:T(8,128)(2,1)S(1)}, bf16[128,128]{1,0:T(8,128)(2,1)S(1)}, u32[]{:S(2)}, u32[]{:S(2)}) %collective-permute-start.9) | collective-permute-done | bytes 32800 | tf_op jit(solution)/shard_map/ppermute | solution.py:172
  154.6 52.5 %while.30 = (s32[]{:T(128)}, f32[2,128]{1,0:T(2,128)S(1)}, f32[2,128]{1,0:T(2,128)}, f32[2,128,128]{2,1,0:T(8,128)S(1)}, bf16[8,128]{1,0:T(8,128)(2,1)}, /*index...) while((s32[]{:T(128)}, f32[2,128]{1,0:T(2,128)S(1)}, ...), condition=%wide.region_7.8_spmd.clone, body=%wide.region_4.7_spmd.clone.sunk | while | flops 17172484 | bytes 840889 | solution.py:219
  154.6 1.2 dynamic_slice.76
  160.6 1.2 dynamic_slice.76
  164.9 1.3 fusion.100
  167.2 1.2 dynamic_slice.76
  171.6 1.3 fusion.100
  173.9 1.2 dynamic_slice.76
  178.2 1.3 fusion.100
  180.5 1.2 dynamic_slice.76
  184.9 1.3 fusion.100
  187.2 1.2 dynamic_slice.76
  191.5 1.3 fusion.100
  193.9 1.2 dynamic_slice.76
  198.2 1.3 fusion.100
  200.5 1.2 dynamic_slice.76
  204.9 1.3 fusion.100
  208.0 2.5 fusion.76
  210.5 27.7 %while.29 = (s32[]{:T(128)}, f32[12,64,256]{2,1,0:T(8,128)}, s32[]{:T(128)}, bf16[8,12]{1,0:T(8,128)(2,1)}, bf16[8,12,64,256]{3,2,1,0:T(8,128)(2,1)}, /*index=5*/s32[]{:T(128)}, s32[]{:T(128)}) while((s32[]{:T(128)}, f32[12,64,256]{2,1,0:T(8,128)}, s32[]{:T(128)}, bf16[8,12]{1,0:T(8,128)(2,1)}, bf16[8,12,64,256]{3,2,1,0:T(8,128)(2,1)}, ...), condition=%wide.region_2.3_spmd.clone, body=%wide.region_1.2_spmd.clone.sunk | while | flops 983056 | bytes 1966305 | solution.py:40
  210.5 1.2 bitcast_convert_fusion.2
  211.7 2.1 fusion.92
  215.0 2.3 fusion.92
  218.4 2.3 fusion.92
  221.9 2.3 fusion.92
  225.4 2.3 fusion.92
  228.9 2.3 fusion.92
  231.2 1.2 bitcast_convert_fusion.2
  232.4 2.3 fusion.92
  234.7 1.2 bitcast_convert_fusion.2
  235.8 2.3 fusion.92
  238.2 1.7 convolution_multiply_fusion.1
  239.9 2.7 %multiply_reduce_fusion = (f32[128,12]{0,1:T(8,128)S(1)}, f32[128,12,64]{0,2,1:T(8,128)S(1)}) fusion(f32[128,12,64]{0,2,1:T(8,128)} %bitcast.91, f32[128,12,64]{0,2,1:T(8,128)S(1)} %convolution_multiply_fusion.1, f32[12,128]{1,0:T(8,128)S(1)} %reduce_window_sum.11, f32[128,128]{1,0:T(8,128)S(1)} %fusion.66, pred[128,128]{1,0:T(8,128)(4,1)} %fusion.64, ...), kind=kOutput, calls=%fused_computation.69 | convolution fusion | flops 152173056 | bytes 1476608 | tf_op jit(solution)/shard_map/htj,jhd->thd/dot_general | solution.py:66
  243.5 1.4 fusion.20
  244.9 19.0 %reduce-scatter.2.cloned.1.call-done = bf16[128,512]{1,0:T(8,128)(2,1)} async-done(((bf16[128,2048]{1,0:T(8,128)(2,1)}), bf16[128,512]{1,0:T(8,128)(2,1)}) %reduce-scatter.2.cloned.1.call-update) | async-done | bytes 131088 | tf_op jit(solution)/shard_map/reduce_scatter | solution.py:230
  (148 shorter events, 55.0 us)
Async XLA Ops:
  6.5 237.0 %copy-start = (bf16[768,2048]{1,0:T(8,128)(2,1)S(1)}, bf16[768,2048]{1,0:T(8,128)(2,1)}, u32[]{:S(2)}) copy-start(bf16[768,2048]{1,0:T(8,128)(2,1)} %param.32) | copy-start | bytes 9437188
  6.5 89.1 %copy-start.6 = (bf16[128,256]{1,0:T(8,128)(2,1)S(1)}, bf16[128,256]{1,0:T(8,128)(2,1)}, u32[]{:S(2)}) copy-start(bf16[128,256]{1,0:T(8,128)(2,1)} %param.28) | copy-start | bytes 196612
  6.5 204.0 %all-gather.5.cloned.1.call-start = ((), (), s32[]{:S(2)}) async-start(), calls=%async_computation.2 | async-start | bytes 3538944 | tf_op jit(solution)/shard_map/all_gather | solution.py:23
  8.8 122.7 %collective-permute-start.3 = (bf16[128,128]{1,0:T(8,128)(2,1)}, bf16[128,128]{1,0:T(8,128)(2,1)}, u32[]{:S(2)}, u32[]{:S(2)}) collective-permute-start(bf16[128,128]{1,0:T(8,128)(2,1)} %get-tuple-element.278), channel_id=1, source_target_pairs={{0,4},{4,8},{8,12},{12,16},{16,20},{20,24},{24,28},{28,0},{1,5},{5... | collective-permute-start | bytes 98312 | tf_op jit(solution)/shard_map/ppermute | solution.py:172
  11.8 121.6 %collective-permute-start.4 = (bf16[128,128]{1,0:T(8,128)(2,1)}, bf16[128,128]{1,0:T(8,128)(2,1)}, u32[]{:S(2)}, u32[]{:S(2)}) collective-permute-start(bf16[128,128]{1,0:T(8,128)(2,1)} %get-tuple-element.278), channel_id=1, source_target_pairs={{0,28},{4,0},{8,4},{12,8},{16,12},{20,16},{24,20},{28,24},{1,29},{... | collective-permute-start | bytes 98312 | tf_op jit(solution)/shard_map/ppermute | solution.py:177
  16.7 81.2 %collective-permute-start.1 = (bf16[3]{0:T(256)(128)(2,1)}, bf16[3]{0:T(256)(128)(2,1)}, u32[]{:S(2)}, u32[]{:S(2)}) collective-permute-start(bf16[3]{0:T(256)(128)(2,1)} %slice.85), channel_id=1, source_target_pairs={{0,4},{4,8},{8,12},{12,16},{16,20},{20,24},{24,28},{1,5},{5,9},{9,... | collective-permute-start | bytes 26 | tf_op jit(solution)/shard_map/ppermute | solution.py:17
  19.8 103.2 %collective-permute-start.2 = (bf16[3,512]{1,0:T(4,128)(2,1)}, bf16[3,512]{1,0:T(4,128)(2,1)}, u32[]{:S(2)}, u32[]{:S(2)}) collective-permute-start(bf16[3,512]{1,0:T(4,128)(2,1)} %slice.95), channel_id=1, source_target_pairs={{0,4},{4,8},{8,12},{12,16},{16,20},{20,24},{24,28},{1,5},{5,9},{9,... | collective-permute-start | bytes 9224 | tf_op jit(solution)/shard_map/ppermute | solution.py:17
  25.4 100.0 %collective-permute-start = (bf16[3,768]{0,1:T(8,128)(2,1)}, bf16[3,768]{0,1:T(8,128)(2,1)}, u32[]{:S(2)}, u32[]{:S(2)}) collective-permute-start(bf16[3,768]{0,1:T(8,128)(2,1)} %copy.27), channel_id=1, source_target_pairs={{0,4},{4,8},{8,12},{12,16},{16,20},{20,24},{24,28},{1,5},{5,9},{9,... | collective-permute-start | bytes 13832 | tf_op jit(solution)/shard_map/ppermute | solution.py:17
  125.2 3.7 %copy-start.2 = (bf16[128,512]{1,0:T(8,128)(2,1)}, bf16[128,512]{1,0:T(8,128)(2,1)S(1)}, u32[]{:S(2)}) copy-start(bf16[128,512]{1,0:T(8,128)(2,1)S(1)} %multiply_convert_fusion.2) | copy-start | bytes 393220
  128.8 0.7 copy-start.4
  131.5 132.5 %reduce-scatter.2.cloned.1.call-start = ((), (), s32[]{:S(2)}) async-start(), calls=%async_computation.1 | async-start | bytes 655360 | tf_op jit(solution)/shard_map/reduce_scatter | solution.py:230
  131.5 7.5 %collective-permute-start.5 = (bf16[128,128]{1,0:T(8,128)(2,1)}, bf16[128,128]{1,0:T(8,128)(2,1)S(1)}, u32[]{:S(2)}, u32[]{:S(2)}) collective-permute-start(bf16[128,128]{1,0:T(8,128)(2,1)} %collective-permute-done.3), channel_id=1, source_target_pairs={{0,4},{4,8},{8,12},{12,16},{16,20},{20,24},{24,28},{28,0},{1,5},{5... | collective-permute-start | bytes 98312 | tf_op jit(solution)/shard_map/ppermute | solution.py:172
  133.4 5.6 %collective-permute-start.6 = (bf16[128,128]{1,0:T(8,128)(2,1)}, bf16[128,128]{1,0:T(8,128)(2,1)S(1)}, u32[]{:S(2)}, u32[]{:S(2)}) collective-permute-start(bf16[128,128]{1,0:T(8,128)(2,1)} %collective-permute-done.4), channel_id=1, source_target_pairs={{0,28},{4,0},{8,4},{12,8},{16,12},{20,16},{24,20},{28,24},{1,29},{... | collective-permute-start | bytes 98312 | tf_op jit(solution)/shard_map/ppermute | solution.py:177
  139.1 7.1 %collective-permute-start.7 = (bf16[128,128]{1,0:T(8,128)(2,1)S(1)}, bf16[128,128]{1,0:T(8,128)(2,1)S(1)}, u32[]{:S(2)}, u32[]{:S(2)}) collective-permute-start(bf16[128,128]{1,0:T(8,128)(2,1)S(1)} %collective-permute-done.5), channel_id=1, source_target_pairs={{0,4},{4,8},{8,12},{12,16},{16,20},{20,24},{24,28},{28,0},{1,5},{5... | collective-permute-start | bytes 98312 | tf_op jit(solution)/shard_map/ppermute | solution.py:172
  139.1 7.7 %collective-permute-start.8 = (bf16[128,128]{1,0:T(8,128)(2,1)S(1)}, bf16[128,128]{1,0:T(8,128)(2,1)S(1)}, u32[]{:S(2)}, u32[]{:S(2)}) collective-permute-start(bf16[128,128]{1,0:T(8,128)(2,1)S(1)} %collective-permute-done.6), channel_id=1, source_target_pairs={{0,28},{4,0},{8,4},{12,8},{16,12},{20,16},{24,20},{28,24},{1,29},{... | collective-permute-start | bytes 98312 | tf_op jit(solution)/shard_map/ppermute | solution.py:177
  146.2 7.3 %collective-permute-start.9 = (bf16[128,128]{1,0:T(8,128)(2,1)S(1)}, bf16[128,128]{1,0:T(8,128)(2,1)S(1)}, u32[]{:S(2)}, u32[]{:S(2)}) collective-permute-start(bf16[128,128]{1,0:T(8,128)(2,1)S(1)} %collective-permute-done.7), channel_id=1, source_target_pairs={{0,4},{4,8},{8,12},{12,16},{16,20},{20,24},{24,28},{28,0},{1,5},{5... | collective-permute-start | bytes 98312 | tf_op jit(solution)/shard_map/ppermute | solution.py:172
  210.5 27.7 %copy-start.3 = (bf16[128,512]{1,0:T(8,128)(2,1)S(1)}, bf16[128,512]{1,0:T(8,128)(2,1)}, u32[]{:S(2)}) copy-start(bf16[128,512]{1,0:T(8,128)(2,1)} %copy-done.2) | copy-start | bytes 393220
  210.5 29.4 %copy-start.5 = (bf16[128,768]{0,1:T(8,128)(2,1)S(1)}, bf16[128,768]{0,1:T(8,128)(2,1)}, u32[]{:S(2)}) copy-start(bf16[128,768]{0,1:T(8,128)(2,1)} %copy-done.4) | copy-start | bytes 589828
  210.5 29.4 %copy-start.7 = (f32[128,12]{0,1:T(8,128)S(1)}, f32[128,12]{0,1:T(8,128)}, u32[]{:S(2)}) copy-start(f32[128,12]{0,1:T(8,128)} %get-tuple-element.283) | copy-start | bytes 18436
  238.2 5.4 %copy-start.1 = (f32[128,2048]{1,0:T(8,128)S(1)}, f32[128,2048]{1,0:T(8,128)}, u32[]{:S(2)}) copy-start(f32[128,2048]{1,0:T(8,128)} %fusion.76) | copy-start | bytes 3145732
Sparse Core Ops, SparseCore 0:
  131.6 59.4 all-gather.4
  245.1 18.8 reduce-scatter.1
